TPU v7x, 512 devices: a whole 4x4x16 slice. The times are simulated.
512 devices in a mesh: ctx: 64 (over z_hi, x, y, core), head: 8 (over z_lo).
Axes of the slice: x: 4, y: 4, z: 16 (z_hi: 2, z_lo: 8; z = z_hi * 8 + z_lo), core: 2. Of those that a mesh axis runs over, the one named last changes fastest.
Arguments:
- query_rows: bfloat16 [32768, 4096], P('ctx', 'head'), may hold values from -32 to 32
- key_rows: bfloat16 [32768, 1024], P('ctx', 'head'), may hold values from -32 to 32
- value_rows: bfloat16 [32768, 1024], P('ctx', 'head'), may hold values from -6 to 6
- out_weight: bfloat16 [4096, 4096], P('head', 'ctx'), may hold values from -0.71875 to 0.71875
Outputs:
- attended: bfloat16 [32768, 4096], P('ctx', 'head')
All inputs are finite; a program needn't handle non-finite values.
Results may differ from a plain program's by a relative error of at most 0.015.
Values may be sent and summed in bfloat16 or wider, within the bound.
A program may use at most 64 MiB of HBM per device.

v0:
```python
import jax
import jax.numpy as jnp
from jax import lax
from jax.sharding import PartitionSpec as P

HD = 128
BLOCK = 512


def from_partner(shard, axis, bit):
    return lax.ppermute(shard, axis, [(i, i ^ 1 << bit) for i in range(lax.axis_size(axis))])


def combine(state, update):
    peak_old, total_old, output_old = state
    peak_new, total_new, output_new = update
    top = jnp.maximum(peak_old, peak_new)
    scale_old = jnp.exp(peak_old - top)
    scale_new = jnp.exp(peak_new - top)
    total = scale_old * total_old + scale_new * total_new
    output = scale_old[..., None] * output_old + scale_new[..., None] * output_new
    return (top, total, output)


def shards(query_rows, key_rows, value_rows, out_weight):
    tok_rows, query_cols = query_rows.shape
    block_count = tok_rows // BLOCK
    heads_kv = key_rows.shape[1] // HD
    heads_query = query_cols // HD
    group = heads_query // heads_kv
    queries = query_rows.reshape(block_count, BLOCK, heads_kv, group, HD)
    stacked = jnp.stack(
        [
            key_rows.reshape(block_count, BLOCK, heads_kv, HD),
            value_rows.reshape(block_count, BLOCK, heads_kv, HD),
        ]
    )
    factor = HD ** (-0.5)

    def block_stats(pair):
        scores = (
            jnp.einsum("bqgrd,bkgd->bgrqk", queries, pair[0], preferred_element_type=jnp.float32)
            * factor
        )
        peak = jnp.max(scores, axis=-1)
        weights = jnp.exp(scores - peak[..., None])
        total = jnp.sum(weights, axis=-1)
        probs = weights.astype(jnp.bfloat16)
        output = jnp.einsum("bgrqk,bkgd->bgrqd", probs, pair[1], preferred_element_type=jnp.float32)
        return (peak, total, output)

    state = block_stats(stacked)
    level_list = list(range(lax.axis_size("ctx").bit_length() - 1))
    for level in level_list:
        partner = from_partner(stacked, "ctx", level)
        state = combine(state, block_stats(partner))
    hidden = state[2] / state[1][..., None]
    hidden = hidden.transpose(0, 3, 1, 2, 4).reshape(tok_rows, query_cols).astype(jnp.bfloat16)
    terms = jnp.dot(
        hidden,
        lax.all_gather(out_weight, "ctx", axis=1, tiled=True),
        preferred_element_type=jnp.float32,
    )
    return lax.psum_scatter(terms.astype(jnp.bfloat16), "head", scatter_dimension=1, tiled=True)


def solution(mesh):
    placed = (P("ctx", "head"), P("ctx", "head"), P("ctx", "head"), P("head", "ctx"))
    return jax.shard_map(
        shards, mesh=mesh, in_specs=placed, out_specs=P("ctx", "head"), check_vma=False
    )
```

profile of v0, /device:TPU:1, one launch (start us, length us, event | category | flops | bytes accessed | tf_op | source)
XLA Modules:
  0.0 273.2 jit_solution(7072032613657819309)
XLA Ops:
  6.5 0.0 copy-start
  6.5 0.0 all-gather.2.cloned.1.call-start
  6.5 0.7 all-gather.2.cloned.1.call-update
  7.3 0.0 reduce-scatter.2.cloned.1.call-start
  7.3 1.0 pad_maximum_fusion
  8.3 3.9 %collective-permute-start.3 = (bf16[2,1,512,1,128]{4,2,3,1,0:T(8,128)(2,1)S(1)}, bf16[2,1,512,1,128]{4,2,3,1,0:T(8,128)(2,1)S(1)}, u32[]{:S(2)}, u32[]{:S(2)}) collective-permute-start(bf16[2,1,512,1,128]{4,2,3,1,0:T(8,128)(2,1)S(1)} %pad_maximum_fusion), channel_id=1, source_target_pairs={{0,64},{8,72},{16,80},{24,88},{32,96},{40,104},{48,112},{56,120},{... | collective-permute-start | bytes 786440 | tf_op jit(solution)/shard_map/ppermute | solution.py:11
  12.3 4.8 %collective-permute-start.2 = (bf16[2,1,512,1,128]{4,2,3,1,0:T(8,128)(2,1)S(1)}, bf16[2,1,512,1,128]{4,2,3,1,0:T(8,128)(2,1)S(1)}, u32[]{:S(2)}, u32[]{:S(2)}) collective-permute-start(bf16[2,1,512,1,128]{4,2,3,1,0:T(8,128)(2,1)S(1)} %pad_maximum_fusion), channel_id=1, source_target_pairs={{0,32},{8,40},{16,48},{24,56},{32,0},{40,8},{48,16},{56,24},{64,96... | collective-permute-start | bytes 786440 | tf_op jit(solution)/shard_map/ppermute | solution.py:11
  17.1 2.3 collective-permute-start.1
  19.4 3.5 %collective-permute-start = (bf16[2,1,512,1,128]{4,2,3,1,0:T(8,128)(2,1)S(1)}, bf16[2,1,512,1,128]{4,2,3,1,0:T(8,128)(2,1)S(1)}, u32[]{:S(2)}, u32[]{:S(2)}) collective-permute-start(bf16[2,1,512,1,128]{4,2,3,1,0:T(8,128)(2,1)S(1)} %pad_maximum_fusion), channel_id=1, source_target_pairs={{0,8},{8,0},{16,24},{24,16},{32,40},{40,32},{48,56},{56,48},{64,72... | collective-permute-start | bytes 786440 | tf_op jit(solution)/shard_map/ppermute | solution.py:11
  22.9 4.3 %collective-permute-start.4 = (bf16[2,1,512,1,128]{4,2,3,1,0:T(8,128)(2,1)S(1)}, bf16[2,1,512,1,128]{4,2,3,1,0:T(8,128)(2,1)S(1)}, u32[]{:S(2)}, u32[]{:S(2)}) collective-permute-start(bf16[2,1,512,1,128]{4,2,3,1,0:T(8,128)(2,1)S(1)} %pad_maximum_fusion), channel_id=1, source_target_pairs={{0,128},{8,136},{16,144},{24,152},{32,160},{40,168},{48,176},{56,1... | collective-permute-start | bytes 786440 | tf_op jit(solution)/shard_map/ppermute | solution.py:11
  27.2 0.0 copy-done
  27.2 1.6 bitcast_reduce_fusion.6
  28.8 0.7 fusion.7
  29.5 0.0 collective-permute-done.1
  29.6 15.4 %collective-permute-start.5 = (bf16[2,1,512,1,128]{4,2,3,1,0:T(8,128)(2,1)S(1)}, bf16[2,1,512,1,128]{4,2,3,1,0:T(8,128)(2,1)S(1)}, u32[]{:S(2)}, u32[]{:S(2)}) collective-permute-start(bf16[2,1,512,1,128]{4,2,3,1,0:T(8,128)(2,1)S(1)} %pad_maximum_fusion), channel_id=1, source_target_pairs={{0,256},{8,264},{16,272},{24,280},{32,288},{40,296},{48,304},{56,3... | collective-permute-start | bytes 786440 | tf_op jit(solution)/shard_map/ppermute | solution.py:11
  45.0 0.7 bitcast_reduce_fusion.4
  45.7 0.7 fusion.11
  46.4 0.0 collective-permute-done.2
  46.5 0.7 bitcast_reduce_fusion.3
  47.2 0.7 fusion.13
  47.9 0.0 collective-permute-done.3
  47.9 0.7 bitcast_reduce_fusion.2
  48.6 0.7 fusion.15
  49.3 0.0 collective-permute-done
  49.3 0.7 bitcast_reduce_fusion.5
  50.1 0.7 fusion.9
  50.8 0.0 collective-permute-done.4
  50.8 0.7 bitcast_reduce_fusion.1
  51.5 0.7 fusion.17
  52.2 0.0 copy-start.1
  52.2 4.7 %collective-permute-done.5 = bf16[2,1,512,1,128]{4,2,3,1,0:T(8,128)(2,1)S(1)} collective-permute-done((bf16[2,1,512,1,128]{4,2,3,1,0:T(8,128)(2,1)S(1)}, bf16[2,1,512,1,128]{4,2,3,1,0:T(8,128)(2,1)S(1)}, u32[]{:S(2)}, u32[]{:S(2)}) %collective-permute-start.5) | collective-permute-done | bytes 262176 | tf_op jit(solution)/shard_map/ppermute | solution.py:11
  56.9 0.7 bitcast_reduce_fusion
  57.7 0.7 fusion.19
  58.4 0.1 multiply_add_fusion
  58.4 0.0 copy-done.1
  58.5 0.9 fusion.56
  59.4 0.9 fusion.77
  60.3 0.9 fusion.80
  61.3 0.9 fusion.83
  62.2 1.1 fusion.86
  63.3 0.9 fusion.89
  64.3 1.7 fusion.113
  66.0 99.9 %all-gather.2.cloned.1.call-done = bf16[512,4096]{0,1:T(8,128)(2,1)} async-done(((bf16[512,64]{0,1:T(8,128)(2,1)}), bf16[512,4096]{0,1:T(8,128)(2,1)}) %all-gather.2.cloned.1.call-update) | async-done | bytes 4194320 | tf_op jit(solution)/shard_map/all_gather | solution.py:61
  165.8 6.6 %convolution_convert_fusion = bf16[512,4096]{1,0:T(8,128)(2,1)} fusion(bf16[512,512]{0,1:T(8,128)(2,1)S(1)} %bitcast.339, bf16[512,4096]{0,1:T(8,128)(2,1)} %all-gather.2.cloned.1.call-done), kind=kOutput, calls=%fused_computation | convolution fusion | flops 2149580800 | bytes 8912896 | tf_op jit(solution)/shard_map/dot_general | solution.py:59
  172.4 0.0 reduce-scatter.2.cloned.1.call-update
  172.4 94.0 %reduce-scatter.2.cloned.1.call-done = bf16[512,512]{1,0:T(8,128)(2,1)} async-done(((bf16[512,4096]{1,0:T(8,128)(2,1)}), bf16[512,512]{1,0:T(8,128)(2,1)}) %reduce-scatter.2.cloned.1.call-update) | async-done | bytes 524304 | tf_op jit(solution)/shard_map/reduce_scatter | solution.py:64
  (1 shorter events, 0.0 us)
Async XLA Ops:
  6.5 20.7 %copy-start = (bf16[512,512]{1,0:T(8,128)(2,1)S(1)}, bf16[512,512]{1,0:T(8,128)(2,1)}, u32[]{:S(2)}) copy-start(bf16[512,512]{1,0:T(8,128)(2,1)} %param.4) | copy-start | bytes 1572868
  6.5 159.3 %all-gather.2.cloned.1.call-start = ((), (), s32[]{:S(2)}) async-start(), calls=%async_computation.1 | async-start | bytes 4259840 | tf_op jit(solution)/shard_map/all_gather | solution.py:61
  7.3 259.1 %reduce-scatter.2.cloned.1.call-start = ((), (), s32[]{:S(2)}) async-start(), calls=%async_computation.2 | async-start | bytes 4718592 | tf_op jit(solution)/shard_map/reduce_scatter | solution.py:64
  8.3 39.6 %collective-permute-start.3 = (bf16[2,1,512,1,128]{4,2,3,1,0:T(8,128)(2,1)S(1)}, bf16[2,1,512,1,128]{4,2,3,1,0:T(8,128)(2,1)S(1)}, u32[]{:S(2)}, u32[]{:S(2)}) collective-permute-start(bf16[2,1,512,1,128]{4,2,3,1,0:T(8,128)(2,1)S(1)} %pad_maximum_fusion), channel_id=1, source_target_pairs={{0,64},{8,72},{16,80},{24,88},{32,96},{40,104},{48,112},{56,120},{... | collective-permute-start | bytes 786440 | tf_op jit(solution)/shard_map/ppermute | solution.py:11
  12.3 34.2 %collective-permute-start.2 = (bf16[2,1,512,1,128]{4,2,3,1,0:T(8,128)(2,1)S(1)}, bf16[2,1,512,1,128]{4,2,3,1,0:T(8,128)(2,1)S(1)}, u32[]{:S(2)}, u32[]{:S(2)}) collective-permute-start(bf16[2,1,512,1,128]{4,2,3,1,0:T(8,128)(2,1)S(1)} %pad_maximum_fusion), channel_id=1, source_target_pairs={{0,32},{8,40},{16,48},{24,56},{32,0},{40,8},{48,16},{56,24},{64,96... | collective-permute-start | bytes 786440 | tf_op jit(solution)/shard_map/ppermute | solution.py:11
  17.1 12.5 %collective-permute-start.1 = (bf16[2,1,512,1,128]{4,2,3,1,0:T(8,128)(2,1)S(1)}, bf16[2,1,512,1,128]{4,2,3,1,0:T(8,128)(2,1)S(1)}, u32[]{:S(2)}, u32[]{:S(2)}) collective-permute-start(bf16[2,1,512,1,128]{4,2,3,1,0:T(8,128)(2,1)S(1)} %pad_maximum_fusion), channel_id=1, source_target_pairs={{0,16},{8,24},{16,0},{24,8},{32,48},{40,56},{48,32},{56,40},{64,80... | collective-permute-start | bytes 786440 | tf_op jit(solution)/shard_map/ppermute | solution.py:11
  19.4 29.9 %collective-permute-start = (bf16[2,1,512,1,128]{4,2,3,1,0:T(8,128)(2,1)S(1)}, bf16[2,1,512,1,128]{4,2,3,1,0:T(8,128)(2,1)S(1)}, u32[]{:S(2)}, u32[]{:S(2)}) collective-permute-start(bf16[2,1,512,1,128]{4,2,3,1,0:T(8,128)(2,1)S(1)} %pad_maximum_fusion), channel_id=1, source_target_pairs={{0,8},{8,0},{16,24},{24,16},{32,40},{40,32},{48,56},{56,48},{64,72... | collective-permute-start | bytes 786440 | tf_op jit(solution)/shard_map/ppermute | solution.py:11
  22.9 27.9 %collective-permute-start.4 = (bf16[2,1,512,1,128]{4,2,3,1,0:T(8,128)(2,1)S(1)}, bf16[2,1,512,1,128]{4,2,3,1,0:T(8,128)(2,1)S(1)}, u32[]{:S(2)}, u32[]{:S(2)}) collective-permute-start(bf16[2,1,512,1,128]{4,2,3,1,0:T(8,128)(2,1)S(1)} %pad_maximum_fusion), channel_id=1, source_target_pairs={{0,128},{8,136},{16,144},{24,152},{32,160},{40,168},{48,176},{56,1... | collective-permute-start | bytes 786440 | tf_op jit(solution)/shard_map/ppermute | solution.py:11
  29.6 27.4 %collective-permute-start.5 = (bf16[2,1,512,1,128]{4,2,3,1,0:T(8,128)(2,1)S(1)}, bf16[2,1,512,1,128]{4,2,3,1,0:T(8,128)(2,1)S(1)}, u32[]{:S(2)}, u32[]{:S(2)}) collective-permute-start(bf16[2,1,512,1,128]{4,2,3,1,0:T(8,128)(2,1)S(1)} %pad_maximum_fusion), channel_id=1, source_target_pairs={{0,256},{8,264},{16,272},{24,280},{32,288},{40,296},{48,304},{56,3... | collective-permute-start | bytes 786440 | tf_op jit(solution)/shard_map/ppermute | solution.py:11
  52.2 6.2 %copy-start.1 = (bf16[512,128]{1,0:T(8,128)(2,1)S(1)}, bf16[512,128]{1,0:T(8,128)(2,1)}, u32[]{:S(2)}) copy-start(bf16[512,128]{1,0:T(8,128)(2,1)} %param.6) | copy-start | bytes 393220
Sparse Core Ops, SparseCore 0:
  11.9 153.8 all-gather.1
  172.5 93.8 reduce-scatter.1
where the time goes:
time: 274 us; the launch traced here: 273 us
  waiting for transfers between devices  199 us (73%)
  starting transfers between devices  34.3 us (13%)
  matrix products  20 us (7%)
  between operations  13.6 us (5%)
  other arithmetic  6 us (2%)
    all_gather x1, waiting for transfers between devices, shards(): lax.all_gather(out_weight, 'ctx', axis=1, tiled=True)  99.9 us
    reduce_scatter x1, waiting for transfers between devices, shards(): lax.psum_scatter(terms.astype(jnp.bfloat16), 'head', scatter_dimension=1,...  94 us
    ppermute x6, starting transfers between devices, from_partner(): lax.ppermute(shard, axis, [(i, i ^ 1 << bit) for i in range(lax.axis_size...  34.3 us
    dot_general x7, matrix products, block_stats(): jnp.einsum('bgrqk,bkgd->bgrqd', probs, pair[1], preferred_element_type=jn...  7.46 us
    dot_general x1, matrix products, shards(): jnp.dot(hidden, lax.all_gather(out_weight, 'ctx', axis=1, tiled=True), pr...  6.56 us
    dot_general x7, matrix products, block_stats(): jnp.einsum('bqgrd,bkgd->bgrqk', queries, pair[0], preferred_element_type=...  5.96 us
  transfers between devices with their start and end apart: 8, of which 3 were waited for; matrix products, arithmetic and copies ran while one was open for 7% of the time, Pallas kernels for 0%

commit v1 on v0

--- a/solution.py
+++ b/solution.py
@@ -58,7 +58,9 @@
     hidden = hidden.transpose(0, 3, 1, 2, 4).reshape(tok_rows, query_cols).astype(jnp.bfloat16)
     terms = jnp.dot(
         hidden,
-        lax.all_gather(out_weight, "ctx", axis=1, tiled=True),
+        jnp.concatenate(
+            lax.all_to_all(jnp.stack([out_weight] * lax.axis_size("ctx")), "ctx", 0, 0), axis=1
+        ),
         preferred_element_type=jnp.float32,
     )
     return lax.psum_scatter(terms.astype(jnp.bfloat16), "head", scatter_dimension=1, tiled=True)

time: 274 us -> 368 us (1.34)
  waiting for transfers between devices: 199 us -> 270 us
  starting transfers between devices: 34.3 us -> 55.4 us
    reduce_scatter x1, waiting for transfers between devices: 94 us -> 196 us  [shards(): lax.psum_scatter(terms.astype(jnp.bfloat16), 'head', scatter_dimension=1,...]
    all_gather x1 -> x0, waiting for transfers between devices: 99.9 us -> none  [shards(): lax.all_gather(out_weight, 'ctx', axis=1, tiled=True)]
    ppermute x6, waiting for transfers between devices: 4.72 us -> 74.6 us  [from_partner(): lax.ppermute(shard, axis, [(i, i ^ 1 << bit) for i in range(lax.axis_size...]
    all_to_all x0 -> x1, starting transfers between devices: none -> 22.6 us  [shards(): lax.all_to_all(jnp.stack([out_weight] * lax.axis_size('ctx')), 'ctx', 0, 0)]
  transfers between devices with their start and end apart: 8 -> 8, of which waited for: 3 -> 3; matrix products, arithmetic and copies ran while one was open for 7% -> 5% of each run, Pallas kernels for 0% -> 0%
where the time goes in v1:
time: 368 us; the launch traced here: 367 us
  waiting for transfers between devices  270 us (73%)
  starting transfers between devices  55.4 us (15%)
  matrix products  19.2 us (5%)
  between operations  13.6 us (4%)
  other arithmetic  5.04 us (1%)
    reduce_scatter x1, waiting for transfers between devices, shards(): lax.psum_scatter(terms.astype(jnp.bfloat16), 'head', scatter_dimension=1,...  196 us
    ppermute x6, waiting for transfers between devices, from_partner(): lax.ppermute(shard, axis, [(i, i ^ 1 << bit) for i in range(lax.axis_size...  74.6 us
    ppermute x6, starting transfers between devices, from_partner(): lax.ppermute(shard, axis, [(i, i ^ 1 << bit) for i in range(lax.axis_size...  32.8 us
    all_to_all x1, starting transfers between devices, shards(): lax.all_to_all(jnp.stack([out_weight] * lax.axis_size('ctx')), 'ctx', 0, 0)  22.6 us
    dot_general x7, matrix products, block_stats(): jnp.einsum('bgrqk,bkgd->bgrqd', probs, pair[1], preferred_element_type=jn...  7.51 us
  transfers between devices with their start and end apart: 8, of which 3 were waited for; matrix products, arithmetic and copies ran while one was open for 5% of the time, Pallas kernels for 0%

profile of v1, /device:TPU:1, one launch (start us, length us, event | category | flops | bytes accessed | tf_op | source)
XLA Modules:
  0.0 367.1 jit_solution(3094345737703187149)
XLA Ops:
  6.5 0.0 copy-start
  6.5 3.4 stack.5
  9.9 0.0 copy-start.1
  9.9 0.0 copy-start.2
  9.9 22.6 %all-to-all-start = ((bf16[64,512,64]{1,2,0:T(8,128)(2,1)}), bf16[64,512,64]{1,2,0:T(8,128)(2,1)}, u32[]{:S(2)}, u32[]{:S(2)}) async-start(bf16[64,512,64]{1,2,0:T(8,128)(2,1)} %stack.5), calls=%async_computation | async-start | bytes 8388608 | tf_op jit(solution)/shard_map/all_to_all | solution.py:62
  32.5 0.0 reduce-scatter.2.cloned.1.call-start
  32.5 0.0 copy-done.1
  32.5 0.0 copy-done.2
  32.6 3.3 collective-permute-start.3
  35.9 4.6 %collective-permute-start.2 = (bf16[2,1,512,1,128]{4,2,3,1,0:T(8,128)(2,1)S(1)}, bf16[2,1,512,1,128]{4,2,3,1,0:T(8,128)(2,1)S(1)}, u32[]{:S(2)}, u32[]{:S(2)}) collective-permute-start(bf16[2,1,512,1,128]{4,2,3,1,0:T(8,128)(2,1)S(1)} %pad_maximum_fusion), channel_id=1, source_target_pairs={{0,32},{8,40},{16,48},{24,56},{32,0},{40,8},{48,16},{56,24},{64,96... | collective-permute-start | bytes 786440 | tf_op jit(solution)/shard_map/ppermute | solution.py:11
  40.5 2.2 collective-permute-start.1
  42.7 3.1 collective-permute-start
  45.8 4.4 %collective-permute-start.4 = (bf16[2,1,512,1,128]{4,2,3,1,0:T(8,128)(2,1)S(1)}, bf16[2,1,512,1,128]{4,2,3,1,0:T(8,128)(2,1)S(1)}, u32[]{:S(2)}, u32[]{:S(2)}) collective-permute-start(bf16[2,1,512,1,128]{4,2,3,1,0:T(8,128)(2,1)S(1)} %pad_maximum_fusion), channel_id=1, source_target_pairs={{0,128},{8,136},{16,144},{24,152},{32,160},{40,168},{48,176},{56,1... | collective-permute-start | bytes 786440 | tf_op jit(solution)/shard_map/ppermute | solution.py:11
  50.2 0.0 copy-done
  50.2 0.7 bitcast_reduce_fusion.6
  50.9 0.7 fusion.7
  51.6 31.9 %collective-permute-done.1 = bf16[2,1,512,1,128]{4,2,3,1,0:T(8,128)(2,1)S(1)} collective-permute-done((bf16[2,1,512,1,128]{4,2,3,1,0:T(8,128)(2,1)S(1)}, bf16[2,1,512,1,128]{4,2,3,1,0:T(8,128)(2,1)S(1)}, u32[]{:S(2)}, u32[]{:S(2)}) %collective-permute-start.1) | collective-permute-done | bytes 262176 | tf_op jit(solution)/shard_map/ppermute | solution.py:11
  83.6 15.3 %collective-permute-start.5 = (bf16[2,1,512,1,128]{4,2,3,1,0:T(8,128)(2,1)S(1)}, bf16[2,1,512,1,128]{4,2,3,1,0:T(8,128)(2,1)S(1)}, u32[]{:S(2)}, u32[]{:S(2)}) collective-permute-start(bf16[2,1,512,1,128]{4,2,3,1,0:T(8,128)(2,1)S(1)} %pad_maximum_fusion), channel_id=1, source_target_pairs={{0,256},{8,264},{16,272},{24,280},{32,288},{40,296},{48,304},{56,3... | collective-permute-start | bytes 786440 | tf_op jit(solution)/shard_map/ppermute | solution.py:11
  98.8 0.7 bitcast_reduce_fusion.4
  99.6 0.7 fusion.11
  100.3 0.0 collective-permute-done.2
  100.3 0.7 bitcast_reduce_fusion.3
  101.0 0.7 fusion.13
  101.7 0.0 collective-permute-done.3
  101.7 0.7 bitcast_reduce_fusion.2
  102.5 0.7 fusion.15
  103.2 0.0 collective-permute-done
  103.2 0.7 bitcast_reduce_fusion.5
  103.9 0.7 fusion.9
  104.6 0.0 collective-permute-done.4
  104.6 0.7 bitcast_reduce_fusion.1
  105.4 0.7 fusion.17
  106.1 42.7 %collective-permute-done.5 = bf16[2,1,512,1,128]{4,2,3,1,0:T(8,128)(2,1)S(1)} collective-permute-done((bf16[2,1,512,1,128]{4,2,3,1,0:T(8,128)(2,1)S(1)}, bf16[2,1,512,1,128]{4,2,3,1,0:T(8,128)(2,1)S(1)}, u32[]{:S(2)}, u32[]{:S(2)}) %collective-permute-start.5) | collective-permute-done | bytes 262176 | tf_op jit(solution)/shard_map/ppermute | solution.py:11
  148.8 0.7 bitcast_reduce_fusion
  149.5 0.7 fusion.19
  150.2 0.1 multiply_add_fusion
  150.3 0.9 fusion.56
  151.2 0.9 fusion.77
  152.2 0.9 fusion.80
  153.1 0.9 fusion.83
  154.1 1.2 fusion.86
  155.2 0.9 fusion.89
  156.2 1.7 fusion.113
  157.9 0.0 all-to-all-done
  157.9 6.6 %convolution_convert_fusion = bf16[512,4096]{1,0:T(8,128)(2,1)} fusion(bf16[512,512]{0,1:T(8,128)(2,1)S(1)} %bitcast.342, bf16[512,4096]{0,1:T(8,128)(2,1)} %bitcast.60), kind=kOutput, calls=%fused_computation | convolution fusion | flops 2149580800 | bytes 8912896 | tf_op jit(solution)/shard_map/dot_general | solution.py:59
  164.4 0.0 reduce-scatter.2.cloned.1.call-update
  164.5 195.8 %reduce-scatter.2.cloned.1.call-done = bf16[512,512]{1,0:T(8,128)(2,1)} async-done(((bf16[512,4096]{1,0:T(8,128)(2,1)}), bf16[512,512]{1,0:T(8,128)(2,1)}) %reduce-scatter.2.cloned.1.call-update) | async-done | bytes 524304 | tf_op jit(solution)/shard_map/reduce_scatter | solution.py:66
  (2 shorter events, 0.0 us)
Async XLA Ops:
  6.5 43.7 %copy-start = (bf16[512,512]{1,0:T(8,128)(2,1)S(1)}, bf16[512,512]{1,0:T(8,128)(2,1)}, u32[]{:S(2)}) copy-start(bf16[512,512]{1,0:T(8,128)(2,1)} %param.4) | copy-start | bytes 1572868
  9.9 22.6 %copy-start.1 = (bf16[512,128]{1,0:T(8,128)(2,1)S(1)}, bf16[512,128]{1,0:T(8,128)(2,1)}, u32[]{:S(2)}) copy-start(bf16[512,128]{1,0:T(8,128)(2,1)} %param.5) | copy-start | bytes 393220
  9.9 22.6 %copy-start.2 = (bf16[512,128]{1,0:T(8,128)(2,1)S(1)}, bf16[512,128]{1,0:T(8,128)(2,1)}, u32[]{:S(2)}) copy-start(bf16[512,128]{1,0:T(8,128)(2,1)} %param.6) | copy-start | bytes 393220
  9.9 147.9 %all-to-all-start = ((bf16[64,512,64]{1,2,0:T(8,128)(2,1)}), bf16[64,512,64]{1,2,0:T(8,128)(2,1)}, u32[]{:S(2)}, u32[]{:S(2)}) async-start(bf16[64,512,64]{1,2,0:T(8,128)(2,1)} %stack.5), calls=%async_computation | async-start | bytes 8388608 | tf_op jit(solution)/shard_map/all_to_all | solution.py:62
  32.5 327.8 %reduce-scatter.2.cloned.1.call-start = ((), (), s32[]{:S(2)}) async-start(), calls=%async_computation.2 | async-start | bytes 4718592 | tf_op jit(solution)/shard_map/reduce_scatter | solution.py:66
  32.6 69.1 %collective-permute-start.3 = (bf16[2,1,512,1,128]{4,2,3,1,0:T(8,128)(2,1)S(1)}, bf16[2,1,512,1,128]{4,2,3,1,0:T(8,128)(2,1)S(1)}, u32[]{:S(2)}, u32[]{:S(2)}) collective-permute-start(bf16[2,1,512,1,128]{4,2,3,1,0:T(8,128)(2,1)S(1)} %pad_maximum_fusion), channel_id=1, source_target_pairs={{0,64},{8,72},{16,80},{24,88},{32,96},{40,104},{48,112},{56,120},{... | collective-permute-start | bytes 786440 | tf_op jit(solution)/shard_map/ppermute | solution.py:11
  35.9 64.4 %collective-permute-start.2 = (bf16[2,1,512,1,128]{4,2,3,1,0:T(8,128)(2,1)S(1)}, bf16[2,1,512,1,128]{4,2,3,1,0:T(8,128)(2,1)S(1)}, u32[]{:S(2)}, u32[]{:S(2)}) collective-permute-start(bf16[2,1,512,1,128]{4,2,3,1,0:T(8,128)(2,1)S(1)} %pad_maximum_fusion), channel_id=1, source_target_pairs={{0,32},{8,40},{16,48},{24,56},{32,0},{40,8},{48,16},{56,24},{64,96... | collective-permute-start | bytes 786440 | tf_op jit(solution)/shard_map/ppermute | solution.py:11
  40.5 43.1 %collective-permute-start.1 = (bf16[2,1,512,1,128]{4,2,3,1,0:T(8,128)(2,1)S(1)}, bf16[2,1,512,1,128]{4,2,3,1,0:T(8,128)(2,1)S(1)}, u32[]{:S(2)}, u32[]{:S(2)}) collective-permute-start(bf16[2,1,512,1,128]{4,2,3,1,0:T(8,128)(2,1)S(1)} %pad_maximum_fusion), channel_id=1, source_target_pairs={{0,16},{8,24},{16,0},{24,8},{32,48},{40,56},{48,32},{56,40},{64,80... | collective-permute-start | bytes 786440 | tf_op jit(solution)/shard_map/ppermute | solution.py:11
  42.7 60.5 %collective-permute-start = (bf16[2,1,512,1,128]{4,2,3,1,0:T(8,128)(2,1)S(1)}, bf16[2,1,512,1,128]{4,2,3,1,0:T(8,128)(2,1)S(1)}, u32[]{:S(2)}, u32[]{:S(2)}) collective-permute-start(bf16[2,1,512,1,128]{4,2,3,1,0:T(8,128)(2,1)S(1)} %pad_maximum_fusion), channel_id=1, source_target_pairs={{0,8},{8,0},{16,24},{24,16},{32,40},{40,32},{48,56},{56,48},{64,72... | collective-permute-start | bytes 786440 | tf_op jit(solution)/shard_map/ppermute | solution.py:11
  45.8 58.8 %collective-permute-start.4 = (bf16[2,1,512,1,128]{4,2,3,1,0:T(8,128)(2,1)S(1)}, bf16[2,1,512,1,128]{4,2,3,1,0:T(8,128)(2,1)S(1)}, u32[]{:S(2)}, u32[]{:S(2)}) collective-permute-start(bf16[2,1,512,1,128]{4,2,3,1,0:T(8,128)(2,1)S(1)} %pad_maximum_fusion), channel_id=1, source_target_pairs={{0,128},{8,136},{16,144},{24,152},{32,160},{40,168},{48,176},{56,1... | collective-permute-start | bytes 786440 | tf_op jit(solution)/shard_map/ppermute | solution.py:11
  83.6 65.2 %collective-permute-start.5 = (bf16[2,1,512,1,128]{4,2,3,1,0:T(8,128)(2,1)S(1)}, bf16[2,1,512,1,128]{4,2,3,1,0:T(8,128)(2,1)S(1)}, u32[]{:S(2)}, u32[]{:S(2)}) collective-permute-start(bf16[2,1,512,1,128]{4,2,3,1,0:T(8,128)(2,1)S(1)} %pad_maximum_fusion), channel_id=1, source_target_pairs={{0,256},{8,264},{16,272},{24,280},{32,288},{40,296},{48,304},{56,3... | collective-permute-start | bytes 786440 | tf_op jit(solution)/shard_map/ppermute | solution.py:11
Sparse Core Ops, SparseCore 0:
  164.6 195.6 reduce-scatter.1
